TPU v7x, 256 devices: a whole 4x4x8 slice. The times are simulated.
256 devices in a mesh: inter: 16 (over x, y), intra: 16 (over z, core).
Axes of the slice: x: 4, y: 4, z: 8, core: 2. Of those that a mesh axis runs over, the one named last changes fastest.
Arguments:
- activations: bfloat16 [131072, 512], P(('inter', 'intra')), may hold values from -24 to 24
- cotangent: bfloat16 [131072, 5120], P(('inter', 'intra')), may hold values from -6 to 6
- counts: int32 [16, 16], P('inter', 'intra'), may hold values from 1 to 4, as said below
- dither_rows: int32 [16, 512], P('inter'), may hold values from 0 to 255
- dither_cols: int32 [16, 5120], P('inter'), may hold values from 0 to 255
- sign_bits: int32 [5120], replicated, may hold values from 0 to 1
Outputs:
- synced: float32 [512, 5120], P('inter')
Inputs may be any that keep to these rules, and one draw needn't show every extreme that they name: Each device processes counts of its 4 microbatch slots; some device has 4 and some device has one in every draw.
All inputs are finite; a program needn't handle non-finite values.
Results may differ from a plain program's by a relative error of at most 0.0003.
Values sent between devices are 32-bit elements; how exact they have to be, the bound alone decides.
A program may use at most 128 MiB of HBM per device.

v0:
```python
import math

import jax
import jax.numpy as jnp
from jax import lax
from jax.sharding import PartitionSpec as P

HBLK = 256
MB = 128


def sylvester(block_len):
    first = jnp.arange(block_len, dtype=jnp.int32)
    parity = jnp.zeros((block_len, block_len), jnp.int32)
    for level in range(block_len.bit_length() - 1):
        parity = parity + first[:, None] // 2**level % 2 * (first[None, :] // 2**level % 2)
    return (1 - 2 * (parity % 2)).astype(jnp.float32)


def rotate_blocks(field, signs_float, hadamard):
    row_count = field.shape[0]
    col_count = field.shape[1]
    block_len = hadamard.shape[0]
    blocks = (field * signs_float).reshape(row_count, col_count // block_len, block_len)
    turned = jnp.einsum(
        "rbk,kl->rbl", blocks, hadamard, precision=lax.Precision.HIGHEST
    ) / math.sqrt(block_len)
    return turned.reshape(row_count, col_count)


def unrotate_blocks(field, signs_float, hadamard):
    row_count = field.shape[0]
    col_count = field.shape[1]
    block_len = hadamard.shape[0]
    blocks = field.reshape(row_count, col_count // block_len, block_len)
    turned = jnp.einsum(
        "rbk,kl->rbl", blocks, hadamard, precision=lax.Precision.HIGHEST
    ) / math.sqrt(block_len)
    return turned.reshape(row_count, col_count) * signs_float


def make_dither(row_terms, col_terms):
    joined = (row_terms[:, None] + col_terms[None, :]) % 256
    return (joined.astype(jnp.float32) + 0.5) / 256.0 - 0.5


def block_peaks(rotated, block_len):
    row_count = rotated.shape[0]
    col_count = rotated.shape[1]
    return jnp.max(jnp.abs(rotated).reshape(row_count, col_count // block_len, block_len), axis=-1)


def encode(rotated, scale, dither):
    row_count = rotated.shape[0]
    col_count = rotated.shape[1]
    nblocks = scale.shape[1]
    scaled = (
        rotated.reshape(row_count, nblocks, col_count // nblocks) / scale[..., None] * 7.5
    ).reshape(row_count, col_count)
    shifted = scaled + dither
    return shifted - jnp.sin(2.0 * math.pi * shifted) / (2.0 * math.pi) - dither


def decode(sums, scale):
    row_count = sums.shape[0]
    col_count = sums.shape[1]
    nblocks = scale.shape[1]
    return (
        sums.reshape(row_count, nblocks, col_count // nblocks) * (scale / 7.5)[..., None]
    ).reshape(row_count, col_count)


def body(activations, cotangent, counts, dither_rows, dither_cols, sign_bits):
    hadamard = sylvester(HBLK)
    signs_float = (1 - 2 * sign_bits).astype(jnp.float32)
    hidden_units = activations.shape[1]
    width = cotangent.shape[1]
    amount = counts[0, 0]

    def accumulate(step, partial_sum):
        left = lax.dynamic_slice_in_dim(activations, step * MB, MB, 0)
        right = lax.dynamic_slice_in_dim(cotangent, step * MB, MB, 0)
        return partial_sum + lax.dot_general(
            left, right, (((0,), (0,)), ((), ())), preferred_element_type=jnp.float32
        )

    gradient = lax.fori_loop(0, amount, accumulate, jnp.zeros((hidden_units, width), jnp.float32))
    gradient = gradient * lax.rsqrt((MB * amount).astype(jnp.float32))
    rotated = rotate_blocks(gradient, signs_float, hadamard)
    scale = lax.pmax(block_peaks(rotated, HBLK), "inter") + 1e-06
    dither = make_dither(dither_rows[0], dither_cols[0])
    codes = encode(rotated, scale, dither)
    pod_count = lax.axis_size("inter")
    share_rows = hidden_units // pod_count
    sums = lax.psum_scatter(codes, "inter", scatter_dimension=0, tiled=True)
    position = lax.axis_index("inter") * share_rows
    scale_share = lax.dynamic_slice_in_dim(scale, position, share_rows, 0)
    decoded = decode(sums, scale_share)
    factor = 1.0 / math.sqrt(pod_count * lax.axis_size("intra"))
    total = lax.psum(decoded, "intra")
    return unrotate_blocks(total, signs_float, hadamard) * factor


def solution(mesh):
    placed = (
        P(("inter", "intra"), None),
        P(("inter", "intra"), None),
        P("inter", "intra"),
        P("inter", None),
        P("inter", None),
        P(),
    )
    return jax.shard_map(
        body, mesh=mesh, in_specs=placed, out_specs=P("inter", None), check_vma=False
    )
```

profile of v0, /device:TPU:1, one launch (start us, length us, event | category | flops | bytes accessed | tf_op | source)
XLA Modules:
  0.0 441.2 jit_solution(5991921151939784352)
XLA Ops:
  6.5 0.0 reduce-scatter.2.cloned.1.call-start
  6.6 0.7 subtract_convert_fusion
  7.9 5.1 %broadcast_in_dim.2 = f32[512,5120]{1,0:T(8,128)} broadcast(f32[]{:T(128)} %constant.306.clone.1), dimensions={} | broadcast | bytes 10485764 | tf_op jit(solution)/shard_map/broadcast_in_dim | solution.py:87
  13.1 11.1 %while.10 = (s32[]{:T(128)}, f32[512,5120]{1,0:T(8,128)}, s32[]{:T(128)}, bf16[512,512]{1,0:T(8,128)(2,1)}, bf16[512,5120]{1,0:T(8,128)(2,1)}, /*index=5*/s32[]{:T(128)}, s32[]{:T(128)}, s32[]{:T(128)}, s32[]{:T(128)}) while((s32[]{:T(128)}, f32[512,5120]{1,0:T(8,128)}, s32[]{:T(128)}, bf16[512,512]{1,0:T(8,128)(2,1)}, ...), condition=%wide.region_1.2_spmd, body=%wide.region_0.1_spmd.sunk | while | flops 673710080 | bytes 22414476 | solution.py:87
  13.7 9.8 %convolution_add_fusion.2 = f32[512,5120]{1,0:T(8,128)} fusion(f32[512,5120]{1,0:T(8,128)} %get-tuple-element.96, bf16[512,5120]{1,0:T(8,128)(2,1)} %get-tuple-element.108, s32[]{:T(128)S(6)} %select_n.378, bf16[512,512]{1,0:T(8,128)(2,1)} %get-tuple-element.107), kind=kOutput, calls=%fused_computation.clone.1 | convolution fusion | flops 673710080 | bytes 22414336 | tf_op jit(solution)/shard_map/while/body/dot_general | solution.py:83
  24.2 11.4 %copy.16 = f32[512,5120]{0,1:T(8,128)} copy(f32[512,5120]{1,0:T(8,128)} %get-tuple-element.33) | data formatting | bytes 20971520 | tf_op jit(solution)/shard_map/while | solution.py:87
  35.6 5.5 %multiply_multiply_fusion = f32[512,5120]{0,1:T(8,128)S(1)} fusion(f32[512,5120]{0,1:T(8,128)} %copy.16, f32[5120]{0:T(1024)S(1)} %subtract_convert_fusion, f32[]{:T(128)S(6)} %rsqrt.3), kind=kLoop, calls=%fused_computation.17 | loop fusion | flops 5242880 | bytes 20992004 | tf_op jit(solution)/shard_map/mul | solution.py:24
  41.2 13.7 %abs_reduce_fusion = (f32[512,20]{0,1:T(8,128)S(1)}, f32[512,20,256]{0,2,1:T(8,128)}) fusion(f32[512,20,256]{0,2,1:T(8,128)S(1)} %bitcast.24, s32[256]{0:T(256)S(1)} %get-tuple-element.46, s32[256]{0:T(256)S(1)} %get-tuple-element.47, s32[256]{0:T(256)S(1)} %get-tuple-element.48, s32[256]{0:T(256)S(1)} %get-tuple-element.49, s32[256]{0:T(256)S(1)} %get-tuple-element.50, ...), kind=kOutput, calls=%fused_computation.16 | convolution fusion | flops 8062818304 | bytes 21020672 | tf_op jit(solution)/shard_map/rbk,kl->rbl/dot_general | solution.py:25
  54.9 78.8 %pmax.7 = f32[512,20]{0,1:T(8,128)S(1)} all-reduce(f32[512,20]{0,1:T(8,128)S(1)} %get-tuple-element.44), channel_id=1, replica_groups=mesh['inter'=16,'intra'=16] {'inter'}, use_global_device_ids=true, to_apply=%region_3.4 | all-reduce | flops 10240 | bytes 81920 | tf_op jit(solution)/shard_map/pmax | solution.py:90
  133.8 9.5 %divide_multiply_fusion = f32[512,20,256]{0,2,1:T(8,128)} fusion(f32[512,20,256]{0,2,1:T(8,128)} %get-tuple-element.45, f32[512,20]{0,1:T(8,128)S(1)} %broadcast_add_fusion), kind=kLoop, calls=%fused_computation.15 | loop fusion | flops 7864320 | bytes 21012480 | tf_op jit(solution)/shard_map/mul | solution.py:58
  143.2 0.0 copy-start
  143.2 0.0 copy-start.1
  143.2 11.5 %copy.19 = f32[512,5120]{1,0:T(8,128)} copy(f32[512,5120]{0,1:T(8,128)} %bitcast.25) | data formatting | bytes 20971520 | tf_op jit(solution)/shard_map/reshape | solution.py:59
  154.7 0.0 copy-done
  154.7 0.0 copy-done.1
  154.7 43.8 %subtract_subtract_fusion = f32[512,5120]{1,0:T(8,128)} fusion(f32[512,5120]{1,0:T(8,128)} %copy.19, s32[5120]{0:T(1024)S(1)} %bitcast.31, s32[512]{0:T(512)S(1)} %bitcast.32), kind=kLoop, calls=%fused_computation.14 | loop fusion | flops 55050240 | bytes 20994048 | tf_op jit(solution)/shard_map/sub | solution.py:61
  198.5 0.0 reduce-scatter.2.cloned.1.call-update
  198.5 0.0 all-reduce.2.cloned.1.call-start
  198.6 0.1 dynamic-slice_multiply_fusion
  198.7 0.1 copy.20
  198.8 0.2 mul.258
  198.9 0.2 copy.28
  199.1 119.3 %reduce-scatter.2.cloned.1.call-done = f32[32,5120]{1,0:T(8,128)} async-done(((f32[512,5120]{1,0:T(8,128)}), f32[32,5120]{1,0:T(8,128)}) %reduce-scatter.2.cloned.1.call-update) | async-done | bytes 655376 | tf_op jit(solution)/shard_map/reduce_scatter | solution.py:95
  318.5 1.2 mul.260
  319.6 0.9 copy.30
  320.5 0.0 all-reduce.2.cloned.1.call-update
  320.6 110.8 %all-reduce.2.cloned.1.call-done = f32[32,20,256]{2,0,1:T(8,128)} async-done(((f32[32,20,256]{2,0,1:T(8,128)}), f32[32,20,256]{2,0,1:T(8,128)}) %all-reduce.2.cloned.1.call-update) | async-done | bytes 655376 | tf_op jit(solution)/shard_map/psum | solution.py:100
  431.3 2.1 fusion.8
  433.5 0.9 multiply_multiply_fusion.1
  (6 shorter events, 0.1 us)
Async XLA Ops:
  6.5 311.9 %reduce-scatter.2.cloned.1.call-start = ((), (), s32[]{:S(2)}) async-start(), calls=%async_computation.1 | async-start | bytes 11141120 | tf_op jit(solution)/shard_map/reduce_scatter | solution.py:95
  143.2 11.5 %copy-start = (s32[1,5120]{1,0:T(1,128)S(1)}, s32[1,5120]{1,0:T(1,128)}, u32[]{:S(2)}) copy-start(s32[1,5120]{1,0:T(1,128)} %param.12) | copy-start | bytes 61444
  143.2 11.5 %copy-start.1 = (s32[1,512]{1,0:T(1,128)S(1)}, s32[1,512]{1,0:T(1,128)}, u32[]{:S(2)}) copy-start(s32[1,512]{1,0:T(1,128)} %param.11) | copy-start | bytes 6148
  198.5 232.8 %all-reduce.2.cloned.1.call-start = ((), (), s32[]{:S(2)}) async-start(), calls=%async_computation.2 | async-start | bytes 1310720 | tf_op jit(solution)/shard_map/psum | solution.py:100
Sparse Core Ops, SparseCore 0:
  198.7 119.7 reduce-scatter.1
  320.8 110.5 all-reduce.1
where the time goes:
time: 440 us; the launch traced here: 441 us
  waiting for transfers between devices  230 us (52%)
  blocking collectives  78.8 us (18%)
  other arithmetic  61.7 us (14%)
  local copies, waits for them, and re-layouts  29.4 us (7%)
  matrix products  25.6 us (6%)
  between operations  14.2 us (3%)
    reduce_scatter x1, waiting for transfers between devices, body(): sums = lax.psum_scatter(codes, 'inter', scatter_dimension=0, tiled=True)  119 us
    psum x1, waiting for transfers between devices, body(): total = lax.psum(decoded, 'intra')  111 us
    pmax x1, blocking collectives, body(): scale = lax.pmax(block_peaks(rotated, HBLK), 'inter') + 1e-06  78.8 us
    sub x1, other arithmetic, encode(): return shifted - jnp.sin(2.0 * math.pi * shifted) / (2.0 * math.pi) - dither  43.8 us
    dot_general x1, matrix products, rotate_blocks(): jnp.einsum('rbk,kl->rbl', blocks, hadamard, precision=lax.Precision.HIGHEST)  13.7 us
    reshape x1, local copies, waits for them, and re-layouts, encode(): scaled = (rotated.reshape(row_count, nblocks, col_count // nblocks) / sca...  11.5 us
    while x1, local copies, waits for them, and re-layouts, body(): lax.fori_loop(0, amount, accumulate, jnp.zeros((hidden_units, width), jnp...  11.4 us
    dot_general x1, matrix products, accumulate(): lax.dot_general(left, right, (((0,), (0,)), ((), ())), preferred_element_...  9.8 us
  transfers between devices with their start and end apart: 2, of which 2 were waited for; matrix products, arithmetic and copies ran while one was open for 0% of the time, Pallas kernels for 0%

commit v1 on v0

v1 whole, which is shorter than its diff:
```python
import math

import jax
import jax.numpy as jnp
from jax import lax
from jax.experimental import pallas as pl
from jax.experimental.pallas import tpu as pltpu
from jax.sharding import PartitionSpec as P

F32 = jnp.float32
BF16 = jnp.bfloat16
HBLK = 256
MB = 128
SIDE = 4
CORES = 2
GROUP = 4
SINE = (
    6.283182621002197,
    -41.34142303466797,
    81.59618377685547,
    -76.5801010131836,
    41.20538330078125,
    -12.27124309539795,
)


def make_kernel(depth, groups):
    cols = groups * GROUP * HBLK

    def kernel(
        counts, drows, dcols, signs, a_hbm, c_hbm, out,
        cbuf, abuf, a2, hmat, colterm, rowterm, rot, pk1, pk2, scl,
        rpx, rpy, rcore, ra, rb, ra2, rb2, stage2, shares, rz, gathered,
        load_sem, s_pk, r_px, r_py, s_core, r_core, s_one, r_a, r_b,
        s_two, r_a2, r_b2, s_z, r_z, s_out, r_out,
    ):
        i_me = lax.axis_index("inter")
        j_me = lax.axis_index("intra")
        x, y = i_me // SIDE, i_me % SIDE
        z, core = j_me // CORES, j_me % CORES
        other = 1 - core

        def at_x(u):
            return (lax.rem(x + u, SIDE) * SIDE + y, j_me)

        def at_y(u):
            return (x * SIDE + lax.rem(y + u, SIDE), j_me)

        def along(axis, u):
            return at_x(u) if axis == 0 else at_y(u)

        def at_z(u, c):
            return (i_me, lax.rem(z + u, depth) * CORES + c)

        sibling = at_z(0, other)

        def put(src, dst, send, recv, device):
            pltpu.make_async_remote_copy(
                src_ref=src, dst_ref=dst, send_sem=send, recv_sem=recv,
                device_id=device, device_id_type=pl.DeviceIdType.MESH,
            ).start()

        def wait_for(ref, sem):
            pltpu.make_async_copy(ref, ref, sem).wait()

        barrier = pltpu.get_barrier_semaphore()
        peers = [at_x(u) for u in range(1, SIDE)] + [at_y(u) for u in range(1, SIDE)]
        peers += [at_z(u, c) for u in range(1, depth) for c in range(CORES)] + [sibling]
        for device in peers:
            pl.semaphore_signal(
                barrier, inc=1, device_id=device, device_id_type=pl.DeviceIdType.MESH
            )

        load_a = pltpu.make_async_copy(a_hbm, abuf, load_sem.at[groups])
        load_a.start()
        width = GROUP * HBLK

        def load_c(g):
            return pltpu.make_async_copy(
                c_hbm.at[:, pl.ds(pl.multiple_of(g * width, width), width)],
                cbuf.at[g], load_sem.at[g],
            )

        for g in range(groups):
            load_c(g).start()

        first = lax.broadcasted_iota(jnp.int32, (HBLK, HBLK), 0)
        second = lax.broadcasted_iota(jnp.int32, (HBLK, HBLK), 1)
        both = first & second
        both = both ^ (both >> 4)
        both = both ^ (both >> 2)
        both = both ^ (both >> 1)
        hmat[...] = (1 - 2 * (both & 1)).astype(F32)

        def turn(tile, carry):
            row = dcols[:, pl.ds(pl.multiple_of(tile * 128, 128), 128)].astype(F32) * (1.0 / 256.0)
            colterm[pl.ds(pl.multiple_of(tile * 128, 128), 128), :] = jnp.broadcast_to(
                row, (128, 128)
            ).T
            return carry

        lax.fori_loop(0, cols // 128, turn, 0)

        load_a.wait()
        amount = counts[0, 0]
        hidden = abuf.shape[1]
        token = lax.broadcasted_iota(jnp.int32, abuf.shape, 0)
        a2[0] = jnp.where(token < amount * MB, abuf[...].astype(F32), 0.0).astype(BF16)
        sub = hidden // (SIDE * SIDE)
        to = lax.broadcasted_iota(jnp.int32, (hidden, hidden), 1)
        source = (to // sub % SIDE) * (SIDE * sub) + to // (SIDE * sub) * sub + to % sub
        fro = lax.broadcasted_iota(jnp.int32, (hidden, hidden), 0)
        order = jnp.where(fro == source, 1.0, 0.0).astype(BF16)
        a2[1] = jnp.dot(a2[0], order, preferred_element_type=F32).astype(BF16)
        row_ints = jnp.broadcast_to(drows[...].astype(F32), (8, hidden))
        rowterm[0] = (row_ints + 0.5) * (1.0 / 256.0)
        row_ints = jnp.dot(row_ints.astype(BF16), order, preferred_element_type=F32)
        rowterm[1] = (row_ints + 0.5) * (1.0 / 256.0)

        counted = jnp.full((1, hidden), amount, jnp.int32)
        weight = jnp.where(counted == 1, 1.0 / math.sqrt(MB), 1.0 / math.sqrt(2 * MB))
        weight = jnp.where(counted == 3, 1.0 / math.sqrt(3 * MB), weight)
        weight = jnp.where(counted == 4, 1.0 / math.sqrt(4 * MB), weight)
        weight = weight * (1.0 / math.sqrt(HBLK))

        def signed(block):
            return (hmat[...] * signs[pl.ds(block, 1), :]).astype(BF16)

        def split(value):
            high = value.astype(BF16)
            return high, (value - high.astype(F32)).astype(BF16)

        def rotate(g):
            load_c(g).wait()
            peaks = []
            for k in range(GROUP):
                block = g * GROUP + k
                grad = lax.dot_general(
                    cbuf[g, :, k * HBLK:(k + 1) * HBLK], a2[k // 2],
                    (((0,), (0,)), ((), ())), preferred_element_type=F32,
                )
                high, low = split(grad)
                turner = signed(block)
                turned = jnp.dot(turner, high, preferred_element_type=F32)
                turned = turned + jnp.dot(turner, low, preferred_element_type=F32)
                turned = turned * weight
                rot[block] = turned
                peaks.append(jnp.max(jnp.abs(turned), axis=0, keepdims=True))
            pk1[g] = jnp.concatenate(peaks + peaks, axis=0)
            for u in range(1, SIDE):
                put(pk1.at[g], rpx.at[g, u - 1], s_pk.at[g, 0], r_px.at[g], at_x(u))

        def peaks_over_y(g):
            wait_for(rpx.at[g], r_px.at[g])
            pk2[g] = jnp.maximum(
                jnp.maximum(pk1[g], rpx[g, 0]), jnp.maximum(rpx[g, 1], rpx[g, 2])
            )
            for u in range(1, SIDE):
                put(pk2.at[g], rpy.at[g, u - 1], s_pk.at[g, 1], r_py.at[g], at_y(u))

        def encode(g, t, c):
            block = g * GROUP + 2 * t + c
            scale = scl[pl.ds(2 * t + c, 1), :]
            up = jnp.broadcast_to(7.5 / scale, (8, scale.shape[1]))
            down = jnp.broadcast_to(scale * (1.0 / (15.0 * math.pi)), up.shape)
            rows = rowterm[t]

            def piece(n, carry):
                at = pl.multiple_of(n * 8, 8)
                value = rot[block, pl.ds(at, 8), :]
                col = colterm[pl.ds(pl.multiple_of(block * HBLK + n * 8, 8), 8), :]
                turns = value * up + (rows + jnp.concatenate([col] * 4, axis=1))
                part = turns - jnp.round(turns)
                square = part * part
                poly = SINE[5] * square + SINE[4]
                for k in (3, 2, 1, 0):
                    poly = poly * square + SINE[k]
                rot[block, pl.ds(at, 8), :] = value + down * (part * poly)
                return carry

            lax.fori_loop(0, HBLK // 8, piece, 0, unroll=4)

        def encode_group(g):
            wait_for(rpy.at[g], r_py.at[g])
            scl[...] = jnp.maximum(
                jnp.maximum(pk2[g], rpy[g, 0]), jnp.maximum(rpy[g, 1], rpy[g, 2])
            ) + 1e-06
            for t in range(2):
                encode(g, t, other)
                put(
                    rot.at[g * GROUP + 2 * t + other], rcore.at[g, t],
                    s_core.at[g, t], r_core.at[g, t], sibling,
                )
            for t in range(2):
                encode(g, t, core)

        half = HBLK // 2

        def lanes(t, u):
            here = x if t == 0 else y
            return pl.ds(pl.multiple_of(lax.rem(here + u, SIDE) * 128, 128), 128)

        top, bottom = pl.ds(0, half), pl.ds(half, half)

        def first_ring(g):
            for t in range(2):
                block = g * GROUP + 2 * t + core
                wait_for(rcore.at[g, t], r_core.at[g, t])
                for n in range(HBLK // 64):
                    rot[block, n * 64:(n + 1) * 64, :] += rcore[g, t, n * 64:(n + 1) * 64, :]
                mine, send = rot.at[block], s_one.at[g, t, 0]
                put(mine.at[top, lanes(t, 2)], ra.at[g, t, 0], send, r_a.at[g, t, 0], along(t, 1))
                put(mine.at[bottom, lanes(t, 2)], ra.at[g, t, 1], send, r_a.at[g, t, 1], along(t, 3))
                put(mine.at[bottom, lanes(t, 1)], rb.at[g, t, 0, bottom], send, r_b.at[g, t, 0], along(t, 1))
                put(mine.at[top, lanes(t, 3)], rb.at[g, t, 1, top], send, r_b.at[g, t, 1], along(t, 3))

        def first_ring_on(g):
            for t in range(2):
                block = g * GROUP + 2 * t + core
                mine, send = rot.at[block], s_one.at[g, t, 1]
                wait_for(ra.at[g, t, 0], r_a.at[g, t, 0])
                rot[block, top, lanes(t, 1)] += ra[g, t, 0]
                put(mine.at[top, lanes(t, 1)], rb.at[g, t, 0, top], send, r_b.at[g, t, 0], along(t, 1))
                wait_for(ra.at[g, t, 1], r_a.at[g, t, 1])
                rot[block, bottom, lanes(t, 3)] += ra[g, t, 1]
                put(mine.at[bottom, lanes(t, 3)], rb.at[g, t, 1, bottom], send, r_b.at[g, t, 1], along(t, 3))

        def rows_of(t, u, part):
            here = y if t == 0 else x
            return pl.ds(pl.multiple_of(lax.rem(here + u, SIDE) * 32 + part * 16, 16), 16)

        def second_ring(g):
            for t in range(2):
                block = g * GROUP + 2 * t + core
                wait_for(rb.at[g, t, 0], r_b.at[g, t, 0])
                wait_for(rb.at[g, t, 1], r_b.at[g, t, 1])
                summed = rot[block, :, lanes(t, 0)] + (rb[g, t, 0] + rb[g, t, 1])
                high, low = split(summed)
                turner = signed(block)
                contract = (((0,), (0,)), ((), ()))
                back = lax.dot_general(high, turner, contract, preferred_element_type=F32)
                back = back + lax.dot_general(low, turner, contract, preferred_element_type=F32)
                stage2[g, t] = back
                mine, send = stage2.at[g, t], s_two.at[g, t, 0]
                put(mine.at[rows_of(t, 2, 0)], ra2.at[g, t, 0], send, r_a2.at[g, t, 0], along(1 - t, 1))
                put(mine.at[rows_of(t, 2, 1)], ra2.at[g, t, 1], send, r_a2.at[g, t, 1], along(1 - t, 3))
                put(mine.at[rows_of(t, 1, 1)], rb2.at[g, t, 0, pl.ds(16, 16)], send, r_b2.at[g, t, 0], along(1 - t, 1))
                put(mine.at[rows_of(t, 3, 0)], rb2.at[g, t, 1, pl.ds(0, 16)], send, r_b2.at[g, t, 1], along(1 - t, 3))

        def second_ring_on(g):
            for t in range(2):
                mine, send = stage2.at[g, t], s_two.at[g, t, 1]
                wait_for(ra2.at[g, t, 0], r_a2.at[g, t, 0])
                stage2[g, t, rows_of(t, 1, 0), :] += ra2[g, t, 0]
                put(mine.at[rows_of(t, 1, 0)], rb2.at[g, t, 0, pl.ds(0, 16)], send, r_b2.at[g, t, 0], along(1 - t, 1))
                wait_for(ra2.at[g, t, 1], r_a2.at[g, t, 1])
                stage2[g, t, rows_of(t, 3, 1), :] += ra2[g, t, 1]
                put(mine.at[rows_of(t, 3, 1)], rb2.at[g, t, 1, pl.ds(16, 16)], send, r_b2.at[g, t, 1], along(1 - t, 3))

        def scatter_z(g):
            for t in range(2):
                wait_for(rb2.at[g, t, 0], r_b2.at[g, t, 0])
                wait_for(rb2.at[g, t, 1], r_b2.at[g, t, 1])
                for part in range(2):
                    summed = stage2[g, t, rows_of(t, 0, part), :] + (
                        rb2[g, t, 0, part * 16:(part + 1) * 16, :]
                        + rb2[g, t, 1, part * 16:(part + 1) * 16, :]
                    )
                    shares[g, 4 * t + 2 * part] = summed[:8]
                    shares[g, 4 * t + 2 * part + 1] = summed[8:]
            for u in range(1, depth):
                put(
                    shares.at[g, lax.rem(z + u, depth)], rz.at[g, u - 1],
                    s_z.at[g], r_z.at[g], at_z(u, core),
                )

        factor = 1.0 / (math.sqrt(HBLK) * math.sqrt(SIDE * SIDE * CORES * depth))

        def gather_z(g):
            wait_for(rz.at[g], r_z.at[g])
            total = shares[g, z]
            for u in range(depth - 1):
                total = total + rz[g, u]
            place = core * depth + z
            gathered[g, place] = total * factor
            for u in range(depth):
                for c in (core, other):
                    if u or c is other:
                        put(
                            gathered.at[g, place], gathered.at[g, place],
                            s_out.at[g], r_out.at[g], at_z(u, c),
                        )

        def deliver(g):
            wait_for(gathered.at[g, pl.ds(0, CORES * depth - 1)], r_out.at[g])
            for k in range(GROUP):
                at = pl.ds(pl.multiple_of((g * GROUP + k) * HBLK, HBLK), HBLK)
                for n in range(4):
                    out[8 * n:8 * n + 8, at] = gathered[g, (k % 2) * depth + 4 * (k // 2) + n]

        def settle(g):
            wait_for(rpx.at[g], s_pk.at[g, 0])
            wait_for(rpy.at[g], s_pk.at[g, 1])
            for t in range(2):
                wait_for(rcore.at[g, t], s_core.at[g, t])
                wait_for(rb.at[g, t], s_one.at[g, t, 0])
                wait_for(ra.at[g, t], s_one.at[g, t, 1])
                wait_for(rb2.at[g, t], s_two.at[g, t, 0])
                wait_for(ra2.at[g, t], s_two.at[g, t, 1])
            wait_for(rz.at[g], s_z.at[g])
            wait_for(gathered.at[g, pl.ds(0, CORES * depth - 1)], s_out.at[g])

        pl.semaphore_wait(barrier, len(peers))

        stages = [
            rotate, peaks_over_y, encode_group, first_ring, first_ring_on,
            second_ring, second_ring_on, scatter_z, gather_z, deliver,
        ]

        def step(s, carry):
            for late in reversed(range(len(stages))):
                g = s - late

                @pl.when((g >= 0) & (g < groups))
                def _(stage=stages[late], g=g):
                    stage(g)

            return carry

        lax.fori_loop(0, groups + len(stages) - 1, step, 0)

        def finish(g, carry):
            settle(g)
            return carry

        lax.fori_loop(0, groups, finish, 0)

    return kernel


def synchronize(depth, counts, dither_rows, dither_cols, signs, activations, cotangent):
    tokens, hidden = activations.shape
    cols = cotangent.shape[1]
    groups = cols // (GROUP * HBLK)
    blocks = groups * GROUP
    dma = pltpu.SemaphoreType.DMA
    vmem = pltpu.VMEM
    share = hidden // (SIDE * SIDE)
    flops = 2 * tokens * hidden * cols + 4 * hidden * cols * HBLK
    return pl.pallas_call(
        make_kernel(depth, groups),
        out_shape=jax.ShapeDtypeStruct((share, cols), F32),
        in_specs=[
            pl.BlockSpec(memory_space=pltpu.SMEM),
            pl.BlockSpec(memory_space=pltpu.VMEM),
            pl.BlockSpec(memory_space=pltpu.VMEM),
            pl.BlockSpec(memory_space=pltpu.VMEM),
            pl.BlockSpec(memory_space=pl.ANY),
            pl.BlockSpec(memory_space=pl.ANY),
        ],
        out_specs=pl.BlockSpec(memory_space=pltpu.VMEM),
        scratch_shapes=[
            vmem((groups, tokens, GROUP * HBLK), BF16),
            vmem((tokens, hidden), BF16),
            vmem((2, tokens, hidden), BF16),
            vmem((HBLK, HBLK), F32),
            vmem((cols, 128), F32),
            vmem((2, 8, hidden), F32),
            vmem((blocks, HBLK, hidden), F32),
            vmem((groups, 8, hidden), F32),
            vmem((groups, 8, hidden), F32),
            vmem((8, hidden), F32),
            vmem((groups, SIDE - 1, 8, hidden), F32),
            vmem((groups, SIDE - 1, 8, hidden), F32),
            vmem((groups, 2, HBLK, hidden), F32),
            vmem((groups, 2, 2, HBLK // 2, 128), F32),
            vmem((groups, 2, 2, HBLK, 128), F32),
            vmem((groups, 2, 2, 16, HBLK), F32),
            vmem((groups, 2, 2, 32, HBLK), F32),
            vmem((groups, 2, 128, HBLK), F32),
            vmem((groups, depth, 8, HBLK), F32),
            vmem((groups, depth - 1, 8, HBLK), F32),
            vmem((groups, CORES * depth, 8, HBLK), F32),
            dma((groups + 1,)),
            dma((groups, 2)),
            dma((groups,)),
            dma((groups,)),
            dma((groups, 2)),
            dma((groups, 2)),
            dma((groups, 2, 2)),
            dma((groups, 2, 2)),
            dma((groups, 2, 2)),
            dma((groups, 2, 2)),
            dma((groups, 2, 2)),
            dma((groups, 2, 2)),
            dma((groups,)),
            dma((groups,)),
            dma((groups,)),
            dma((groups,)),
        ],
        compiler_params=pltpu.CompilerParams(
            collective_id=0, has_side_effects=True, vmem_limit_bytes=56 * 2**20
        ),
        cost_estimate=pl.CostEstimate(
            flops=flops, bytes_accessed=2 * tokens * (hidden + cols), transcendentals=0
        ),
    )(counts, dither_rows, dither_cols, signs, activations, cotangent)


def solution(mesh):
    depth = mesh.shape["intra"] // CORES

    def body(activations, cotangent, counts, dither_rows, dither_cols, sign_bits):
        signs = (1 - 2 * sign_bits).astype(F32).reshape(-1, HBLK)
        return synchronize(
            depth, counts, dither_rows, dither_cols, signs, activations, cotangent
        )

    placed = (
        P(("inter", "intra"), None),
        P(("inter", "intra"), None),
        P("inter", "intra"),
        P("inter", None),
        P("inter", None),
        P(),
    )
    return jax.shard_map(
        body, mesh=mesh, in_specs=placed, out_specs=P("inter", None), check_vma=False
    )
```

time: 440 us -> 98 us (0.22)
  waiting for transfers between devices: 230 us -> 0 us
  Pallas kernels: 0 us -> 93.8 us
  blocking collectives: 78.8 us -> 0 us
  other arithmetic: 61.7 us -> 0.73 us
  local copies, waits for them, and re-layouts: 29.4 us -> 2.58 us
  matrix products: 25.6 us -> 0 us
  between operations: 14.2 us -> 0.66 us
    reduce_scatter x1 -> x0, waiting for transfers between devices: 119 us -> none  [body(): sums = lax.psum_scatter(codes, 'inter', scatter_dimension=0, tiled=True)]
    psum x1 -> x0, waiting for transfers between devices: 111 us -> none  [body(): total = lax.psum(decoded, 'intra')]
    pallas_call x0 -> x1, Pallas kernels: none -> 93.8 us  [synchronize(): pl.pallas_call(make_kernel(depth, groups), out_shape=jax.ShapeDtypeStruct...]
    pmax x1 -> x0, blocking collectives: 78.8 us -> none  [body(): scale = lax.pmax(block_peaks(rotated, HBLK), 'inter') + 1e-06]
    sub x1 -> x0, other arithmetic: 43.8 us -> none  [encode(): return shifted - jnp.sin(2.0 * math.pi * shifted) / (2.0 * math.pi) - dither]
    dot_general x3 -> x0, matrix products: 25.6 us -> none  [the longest x1 13.7 us: rotate_blocks(): jnp.einsum('rbk,kl->rbl', blocks, hadamard, precision=lax.Precision.HIGHEST)]
    mul x4 -> x0, other arithmetic: 17.1 us -> none  [the longest x1 9.48 us: encode(): rotated.reshape(row_count, nblocks, col_count // nblocks) / scale[..., None]]
    reshape x3 -> x1, local copies, waits for them, and re-layouts: 12.4 us -> 0.62 us  [body(): signs = (1 - 2 * sign_bits).astype(F32).reshape(-1, HBLK)]
  transfers between devices with their start and end apart: 2 -> 0, of which waited for: 2 -> 0; matrix products, arithmetic and copies ran while one was open for 0% -> 0% of each run, Pallas kernels for 0% -> 0%
where the time goes in v1:
time: 98 us; the launch traced here: 97.8 us
  Pallas kernels  93.8 us (96%)
  local copies, waits for them, and re-layouts  2.58 us (3%)
    pallas_call x1, Pallas kernels, synchronize(): pl.pallas_call(make_kernel(depth, groups), out_shape=jax.ShapeDtypeStruct...  93.8 us
    unnamed x1, local copies, waits for them, and re-layouts  1.97 us

profile of v1, /device:TPU:1, one launch (start us, length us, event | category | flops | bytes accessed | tf_op | source)
XLA Modules:
  0.0 97.8 jit_solution(10155485973602876849)
XLA Ops:
  0.7 0.7 subtract_convert_fusion
  1.4 0.6 reshape.3.signs
  2.0 93.8 %shard_map.64 = f32[32,5120]{1,0:T(8,128)} custom-call(s32[1,1]{1,0:T(1,128)S(6)} %copy.8.counts, s32[1,512]{1,0:T(1,128)} %drows.1, s32[1,5120]{1,0:T(1,128)} %dcols.1, f32[20,256]{1,0:T(8,128)} %reshape.3.signs, bf16[512,512]{1,0:T(8,128)(2,1)} %a_hbm.1, bf16[512,5120]{1,0:T(8,128)(2,1)} %c_hbm.1), custom_call_target="tpu_custom_call" | custom-call | flops 5368709120 | bytes 5767168 | tf_op jit(solution)/shard_map/pallas_call | solution.py:350
  95.8 2.0 %copy.9 = f32[32,5120]{1,0:T(8,128)} copy(f32[32,5120]{1,0:T(8,128)} %shard_map.64) | data formatting | bytes 1310720

commit v2 on v1

v2 whole, which is shorter than its diff:
```python
import math

import jax
import jax.numpy as jnp
from jax import lax
from jax.experimental import pallas as pl
from jax.experimental.pallas import tpu as pltpu
from jax.sharding import PartitionSpec as P

F32 = jnp.float32
BF16 = jnp.bfloat16
HBLK = 256
MB = 128
SIDE = 4
CORES = 2
GROUP = 4
LEAD = 32.78138732910156
SINE = tuple(c / LEAD for c in (
    6.283055782318115, -41.331214904785156, 81.36681365966797, -74.47799682617188,
))


def make_kernel(depth, groups):
    cols = groups * GROUP * HBLK

    def kernel(
        counts, drows, dcols, signs, a_hbm, c_hbm, out,
        cbuf, abuf, a2, hmat, colterm, rowterm, rot, pk1, pk2, scl,
        rplane, rpx, rpy, rcore, ra, rb, rb2, stage2, shares, rz, gathered,
        load_sem, s_pk, r_px, r_py, s_core, r_core, s_one, r_a, r_b,
        s_two, r_b2, s_z, r_z, s_out, r_out, s_pair, r_pair,
    ):
        i_me = lax.axis_index("inter")
        j_me = lax.axis_index("intra")
        x, y = i_me // SIDE, i_me % SIDE
        z, core = j_me // CORES, j_me % CORES
        other = 1 - core

        def at_x(u):
            return (lax.rem(x + u, SIDE) * SIDE + y, j_me)

        def at_y(u):
            return (x * SIDE + lax.rem(y + u, SIDE), j_me)

        def at_plane(u, v):
            return (lax.rem(x + u, SIDE) * SIDE + lax.rem(y + v, SIDE), j_me)

        def along(axis, u):
            to_x = lax.rem(x + u * (1 - axis), SIDE)
            to_y = lax.rem(y + u * axis, SIDE)
            return (to_x * SIDE + to_y, j_me)

        def at_z(u, c):
            return (i_me, lax.rem(z + u, depth) * CORES + c)

        sibling = at_z(0, other)

        def put(src, dst, send, recv, device):
            pltpu.make_async_remote_copy(
                src_ref=src, dst_ref=dst, send_sem=send, recv_sem=recv,
                device_id=device, device_id_type=pl.DeviceIdType.MESH,
            ).start()

        def wait_for(ref, sem):
            pltpu.make_async_copy(ref, ref, sem).wait()

        barrier = pltpu.get_barrier_semaphore()
        plane = [(u, v) for u in range(SIDE) for v in range(SIDE) if u or v]
        peers = [at_plane(u, v) for u, v in plane]
        peers += [at_z(u, core) for u in range(1, depth)] + [sibling]
        for device in peers:
            pl.semaphore_signal(
                barrier, inc=1, device_id=device, device_id_type=pl.DeviceIdType.MESH
            )

        load_a = pltpu.make_async_copy(a_hbm, abuf, load_sem.at[groups])
        load_a.start()
        width = GROUP * HBLK

        def load_c(g):
            return pltpu.make_async_copy(
                c_hbm.at[:, pl.ds(pl.multiple_of(g * width, width), width)],
                cbuf.at[g], load_sem.at[g],
            )

        for g in range(groups):
            load_c(g).start()

        first = lax.broadcasted_iota(jnp.int32, (HBLK, HBLK), 0)
        second = lax.broadcasted_iota(jnp.int32, (HBLK, HBLK), 1)
        both = first & second
        both = both ^ (both >> 4)
        both = both ^ (both >> 2)
        both = both ^ (both >> 1)
        hmat[...] = (1 - 2 * (both & 1)).astype(F32)

        load_a.wait()
        amount = counts[0, 0]
        hidden = abuf.shape[1]
        token = lax.broadcasted_iota(jnp.int32, abuf.shape, 0)
        a2[0] = jnp.where(token < amount * MB, abuf[...].astype(F32), 0.0).T.astype(BF16)
        sub = hidden // (SIDE * SIDE)
        for u in range(SIDE):
            for v in range(SIDE):
                a2[1, pl.ds((v * SIDE + u) * sub, sub), :] = a2[0, pl.ds((u * SIDE + v) * sub, sub), :]

        def dither_terms():
            def turn(tile, carry):
                at = pl.multiple_of(tile * 128, 128)
                row = dcols[:, pl.ds(at, 128)].astype(F32) * (1.0 / 256.0)
                colterm[pl.ds(at, 128), :] = jnp.broadcast_to(row, (128, 128)).T
                return carry

            lax.fori_loop(0, cols // 128, turn, 0, unroll=8)
            row_ints = jnp.broadcast_to(drows[...].astype(F32), (8, hidden))
            rowterm[0] = (row_ints + 0.5) * (1.0 / 256.0)
            to = lax.broadcasted_iota(jnp.int32, (hidden, hidden), 1)
            source = (to // sub % SIDE) * (SIDE * sub) + to // (SIDE * sub) * sub + to % sub
            fro = lax.broadcasted_iota(jnp.int32, (hidden, hidden), 0)
            order = jnp.where(fro == source, 1.0, 0.0).astype(BF16)
            row_ints = jnp.dot(row_ints.astype(BF16), order, preferred_element_type=F32)
            rowterm[1] = (row_ints + 0.5) * (1.0 / 256.0)

        counted = jnp.full((1, hidden), amount, jnp.int32)
        weight = jnp.where(counted == 1, 1.0 / math.sqrt(MB), 1.0 / math.sqrt(2 * MB))
        weight = jnp.where(counted == 3, 1.0 / math.sqrt(3 * MB), weight)
        weight = jnp.where(counted == 4, 1.0 / math.sqrt(4 * MB), weight)
        weight = weight * (1.0 / math.sqrt(HBLK))

        def signed(block):
            bits = signs[pl.ds(pl.multiple_of(block * HBLK, HBLK), HBLK)].reshape(1, HBLK)
            return (hmat[...] * (1 - 2 * bits).astype(F32)).astype(BF16)

        def split(value):
            high = value.astype(BF16)
            return high, (value - high.astype(F32)).astype(BF16)

        def rotate(g):
            load_c(g).wait()
            peaks = []
            for k in range(GROUP):
                block = g * GROUP + k
                grad = jnp.dot(
                    a2[k // 2], cbuf[g, :, k * HBLK:(k + 1) * HBLK], preferred_element_type=F32
                )
                high, low = split(grad)
                turner = signed(block)
                lasts = (((1,), (1,)), ((), ()))
                turned = lax.dot_general(turner, high, lasts, preferred_element_type=F32)
                turned = turned + lax.dot_general(turner, low, lasts, preferred_element_type=F32)
                turned = turned * weight
                rot[block] = turned
                peaks.append(jnp.max(jnp.abs(turned), axis=0, keepdims=True))
            pk1[g] = jnp.concatenate(peaks + peaks, axis=0)

            @pl.when(g == 0)
            def _():
                pl.semaphore_wait(barrier, len(peers))

            @pl.when(g == 0)
            def _():
                for k, (u, v) in enumerate(plane):
                    put(pk1.at[0], rplane.at[k], s_pk.at[0, 0], r_px.at[0], at_plane(u, v))

            @pl.when(g > 0)
            def _():
                for u in range(1, SIDE):
                    put(pk1.at[g], rpx.at[g, u - 1], s_pk.at[g, 0], r_px.at[g], at_x(u))

        def peaks_over_y(g):
            wait_for(rpx.at[g], r_px.at[g])
            pk2[g] = jnp.maximum(
                jnp.maximum(pk1[g], rpx[g, 0]), jnp.maximum(rpx[g, 1], rpx[g, 2])
            )
            for u in range(1, SIDE):
                put(pk2.at[g], rpy.at[g, u - 1], s_pk.at[g, 1], r_py.at[g], at_y(u))

        def encode(g, t, c):
            block = g * GROUP + 2 * t + c
            scale = scl[pl.ds(2 * t + c, 1), :]
            up = jnp.broadcast_to(7.5 / scale, (8, scale.shape[1]))
            down = jnp.broadcast_to(scale * (LEAD / (15.0 * math.pi)), up.shape)
            rows = rowterm[t]

            def piece(n, carry):
                at = pl.multiple_of(n * 8, 8)
                value = rot[block, pl.ds(at, 8), :]
                col = colterm[pl.ds(pl.multiple_of(block * HBLK + n * 8, 8), 8), :]
                turns = value * up + (rows + jnp.concatenate([col] * 4, axis=1))
                part = turns - jnp.round(turns)
                square = part * part
                poly = square + SINE[3]
                for k in (2, 1, 0):
                    poly = poly * square + SINE[k]
                rot[block, pl.ds(at, 8), :] = value + down * (part * poly)
                return carry

            lax.fori_loop(0, HBLK // 8, piece, 0, unroll=4)

        def scales(g):
            @pl.when(g == 0)
            def _():
                wait_for(rplane, r_px.at[0])
                top_peaks = pk1[0]
                for k in range(len(plane)):
                    top_peaks = jnp.maximum(top_peaks, rplane[k])
                scl[...] = top_peaks + 1e-06

            @pl.when(g > 0)
            def _():
                wait_for(rpy.at[g], r_py.at[g])
                scl[...] = jnp.maximum(
                    jnp.maximum(pk2[g], rpy[g, 0]), jnp.maximum(rpy[g, 1], rpy[g, 2])
                ) + 1e-06

        def encode_other(g, t):
            encode(g, t, other)
            put(
                rot.at[g * GROUP + 2 * t + other], rcore.at[g, t],
                s_core.at[g, t], r_core.at[g, t], sibling,
            )

        def encode_own(g, t):
            encode(g, t, core)

        half = HBLK // 2

        def lanes(t, u):
            here = x + t * (y - x)
            return pl.ds(pl.multiple_of(lax.rem(here + u, SIDE) * 128, 128), 128)

        top, bottom = pl.ds(0, half), pl.ds(half, half)

        def first_ring(g, t):
            block = g * GROUP + 2 * t + core
            wait_for(rcore.at[g, t], r_core.at[g, t])
            for n in range(HBLK // 64):
                rot[block, n * 64:(n + 1) * 64, :] += rcore[g, t, n * 64:(n + 1) * 64, :]
            mine, send = rot.at[block], s_one.at[g, t, 0]
            put(mine.at[top, lanes(t, 2)], ra.at[g, t, 0], send, r_a.at[g, t, 0], along(t, 1))
            put(mine.at[bottom, lanes(t, 2)], ra.at[g, t, 1], send, r_a.at[g, t, 1], along(t, 3))
            put(mine.at[bottom, lanes(t, 1)], rb.at[g, t, 0, bottom], send, r_b.at[g, t, 0], along(t, 1))
            put(mine.at[top, lanes(t, 3)], rb.at[g, t, 1, top], send, r_b.at[g, t, 1], along(t, 3))

        def first_ring_on(g, t):
            block = g * GROUP + 2 * t + core
            mine, send = rot.at[block], s_one.at[g, t, 1]
            wait_for(ra.at[g, t, 0], r_a.at[g, t, 0])
            rot[block, top, lanes(t, 1)] += ra[g, t, 0]
            put(mine.at[top, lanes(t, 1)], rb.at[g, t, 0, top], send, r_b.at[g, t, 0], along(t, 1))
            wait_for(ra.at[g, t, 1], r_a.at[g, t, 1])
            rot[block, bottom, lanes(t, 3)] += ra[g, t, 1]
            put(mine.at[bottom, lanes(t, 3)], rb.at[g, t, 1, bottom], send, r_b.at[g, t, 1], along(t, 3))

        def rows_of(t, u):
            here = y + t * (x - y)
            return pl.ds(pl.multiple_of(lax.rem(here + u, SIDE) * 32, 32), 32)

        def second_ring(g, t):
            block = g * GROUP + 2 * t + core
            wait_for(rb.at[g, t, 0], r_b.at[g, t, 0])
            wait_for(rb.at[g, t, 1], r_b.at[g, t, 1])
            summed = rot[block, :, lanes(t, 0)] + (rb[g, t, 0] + rb[g, t, 1])
            high, low = split(summed)
            turner = signed(block)
            contract = (((0,), (0,)), ((), ()))
            back = lax.dot_general(high, turner, contract, preferred_element_type=F32)
            back = back + lax.dot_general(low, turner, contract, preferred_element_type=F32)
            stage2[g, t] = back
            mine, send = stage2.at[g, t], s_two.at[g, t]
            for u in range(1, SIDE):
                put(mine.at[rows_of(t, u)], rb2.at[g, t, u - 1], send, r_b2.at[g, t], along(1 - t, u))

        def second_sum(g, t):
            wait_for(rb2.at[g, t], r_b2.at[g, t])
            summed = (stage2[g, t, rows_of(t, 0), :] + rb2[g, t, 0]) + (rb2[g, t, 1] + rb2[g, t, 2])
            for n in range(4):
                shares[g, 4 * t + n] = summed[8 * n:8 * n + 8]

        def scatter_z(g):
            for u in range(1, depth):
                put(
                    shares.at[g, lax.rem(z + u, depth)], rz.at[g, u - 1],
                    s_z.at[g], r_z.at[g], at_z(u, core),
                )

        def gather_z(g):
            wait_for(rz.at[g], r_z.at[g])
            total = shares[g, z]
            for u in range(depth - 1):
                total = total + rz[g, u]
            place = core * depth + z
            gathered[g, place] = total
            for u in range(1, depth):
                put(
                    gathered.at[g, place], gathered.at[g, place],
                    s_out.at[g], r_out.at[g], at_z(u, core),
                )

        def half_of(g, c):
            return gathered.at[g, pl.ds(c * depth, depth)]

        def share_core(g):
            wait_for(rz.at[g], r_out.at[g])
            put(half_of(g, core), half_of(g, core), s_pair.at[g], r_pair.at[g], sibling)

        def deliver(g):
            wait_for(half_of(g, other), r_pair.at[g])
            for k in range(GROUP):
                at = pl.ds(pl.multiple_of((g * GROUP + k) * HBLK, HBLK), HBLK)
                for n in range(4):
                    out[8 * n:8 * n + 8, at] = gathered[g, (k % 2) * depth + 4 * (k // 2) + n]

        def settle(g):
            @pl.when(g == 0)
            def _():
                wait_for(rplane, s_pk.at[0, 0])

            @pl.when(g > 0)
            def _():
                wait_for(rpx.at[g], s_pk.at[g, 0])
                wait_for(rpy.at[g], s_pk.at[g, 1])

            for t in range(2):
                wait_for(rcore.at[g, t], s_core.at[g, t])
                wait_for(rb.at[g, t], s_one.at[g, t, 0])
                wait_for(ra.at[g, t], s_one.at[g, t, 1])
                wait_for(rb2.at[g, t], s_two.at[g, t])
            wait_for(rz.at[g], s_z.at[g])
            wait_for(rz.at[g], s_out.at[g])
            wait_for(half_of(g, core), s_pair.at[g])

        def at_step(g, stage):
            @pl.when((g >= 0) & (g < groups))
            def _():
                stage(g)

        def at_half(h, stage):
            @pl.when((h >= 0) & (h < 2 * groups))
            def _():
                stage(h // 2, h % 2)

        def after_pair(h, stage):
            @pl.when((h >= 0) & (h < 2 * groups) & (h % 2 == 1))
            def _():
                stage(h // 2)

        def before_pair(h, stage):
            @pl.when((h >= 0) & (h < 2 * groups) & (h % 2 == 0))
            def _():
                stage(h // 2)

        ahead = 2

        def early(s, carry):
            rotate(s)

            @pl.when(s > ahead)
            def _():
                peaks_over_y(s - ahead)

            return carry

        lax.fori_loop(0, groups, early, 0)
        dither_terms()

        def late(s, carry):
            before_pair(s + 2 * (groups - ahead), peaks_over_y)
            before_pair(s, scales)
            at_half(s, encode_other)
            at_half(s, encode_own)
            at_half(s - 1, first_ring)
            at_half(s - 4, first_ring_on)
            at_half(s - 7, second_ring)
            at_half(s - 9, second_sum)
            after_pair(s - 9, scatter_z)
            after_pair(s - 12, gather_z)
            after_pair(s - 15, share_core)
            return carry

        lax.fori_loop(0, 2 * groups + 15, late, 0)

        def finish(g, carry):
            deliver(g)
            settle(g)
            return carry

        lax.fori_loop(0, groups, finish, 0)

    return kernel


def synchronize(depth, counts, dither_rows, dither_cols, signs, activations, cotangent):
    tokens, hidden = activations.shape
    cols = cotangent.shape[1]
    groups = cols // (GROUP * HBLK)
    blocks = groups * GROUP
    dma = pltpu.SemaphoreType.DMA
    vmem = pltpu.VMEM
    share = hidden // (SIDE * SIDE)
    flops = 2 * tokens * hidden * cols + 4 * hidden * cols * HBLK
    return pl.pallas_call(
        make_kernel(depth, groups),
        out_shape=jax.ShapeDtypeStruct((share, cols), F32),
        in_specs=[
            pl.BlockSpec(memory_space=pltpu.SMEM),
            pl.BlockSpec(memory_space=pltpu.VMEM),
            pl.BlockSpec(memory_space=pltpu.VMEM),
            pl.BlockSpec(memory_space=pltpu.VMEM),
            pl.BlockSpec(memory_space=pl.ANY),
            pl.BlockSpec(memory_space=pl.ANY),
        ],
        out_specs=pl.BlockSpec(memory_space=pltpu.VMEM),
        scratch_shapes=[
            vmem((groups, tokens, GROUP * HBLK), BF16),
            vmem((tokens, hidden), BF16),
            vmem((2, hidden, tokens), BF16),
            vmem((HBLK, HBLK), F32),
            vmem((cols, 128), F32),
            vmem((2, 8, hidden), F32),
            vmem((blocks, HBLK, hidden), F32),
            vmem((groups, 8, hidden), F32),
            vmem((groups, 8, hidden), F32),
            vmem((8, hidden), F32),
            vmem((SIDE * SIDE - 1, 8, hidden), F32),
            vmem((groups, SIDE - 1, 8, hidden), F32),
            vmem((groups, SIDE - 1, 8, hidden), F32),
            vmem((groups, 2, HBLK, hidden), F32),
            vmem((groups, 2, 2, HBLK // 2, 128), F32),
            vmem((groups, 2, 2, HBLK, 128), F32),
            vmem((groups, 2, SIDE - 1, 32, HBLK), F32),
            vmem((groups, 2, 128, HBLK), F32),
            vmem((groups, depth, 8, HBLK), F32),
            vmem((groups, depth - 1, 8, HBLK), F32),
            vmem((groups, CORES * depth, 8, HBLK), F32),
            dma((groups + 1,)),
            dma((groups, 2)),
            dma((groups,)),
            dma((groups,)),
            dma((groups, 2)),
            dma((groups, 2)),
            dma((groups, 2, 2)),
            dma((groups, 2, 2)),
            dma((groups, 2, 2)),
            dma((groups, 2)),
            dma((groups, 2)),
            dma((groups,)),
            dma((groups,)),
            dma((groups,)),
            dma((groups,)),
            dma((groups,)),
            dma((groups,)),
        ],
        compiler_params=pltpu.CompilerParams(
            collective_id=0, has_side_effects=True, vmem_limit_bytes=56 * 2**20
        ),
        cost_estimate=pl.CostEstimate(
            flops=flops, bytes_accessed=2 * tokens * (hidden + cols), transcendentals=0
        ),
    )(counts, dither_rows, dither_cols, signs, activations, cotangent)


def solution(mesh):
    depth = mesh.shape["intra"] // CORES

    def body(activations, cotangent, counts, dither_rows, dither_cols, sign_bits):
        summed = synchronize(
            depth, counts, dither_rows, dither_cols, sign_bits, activations, cotangent
        )
        return summed * (1.0 / (math.sqrt(HBLK) * math.sqrt(mesh.size)))

    placed = (
        P(("inter", "intra"), None),
        P(("inter", "intra"), None),
        P("inter", "intra"),
        P("inter", None),
        P("inter", None),
        P(),
    )
    return jax.shard_map(
        body, mesh=mesh, in_specs=placed, out_specs=P("inter", None), check_vma=False
    )
```

time: 98 us -> 75.5 us (0.77)
  Pallas kernels: 93.8 us -> 72.7 us
  local copies, waits for them, and re-layouts: 2.58 us -> 0 us
  other arithmetic: 0.73 us -> 1.97 us
    pallas_call x1, Pallas kernels: 93.8 us -> 72.7 us  [synchronize(): pl.pallas_call(make_kernel(depth, groups), out_shape=jax.ShapeDtypeStruct...]
    mul x0 -> x1, other arithmetic: none -> 1.97 us  [body(): return summed * (1.0 / (math.sqrt(HBLK) * math.sqrt(mesh.size)))]
    unnamed x1 -> x0, local copies, waits for them, and re-layouts: 1.97 us -> none
where the time goes in v2:
time: 75.5 us; the launch traced here: 75.3 us
  Pallas kernels  72.7 us (96%)
  other arithmetic  1.97 us (3%)
    pallas_call x1, Pallas kernels, synchronize(): pl.pallas_call(make_kernel(depth, groups), out_shape=jax.ShapeDtypeStruct...  72.7 us
    mul x1, other arithmetic, body(): return summed * (1.0 / (math.sqrt(HBLK) * math.sqrt(mesh.size)))  1.97 us

profile of v2, /device:TPU:1, one launch (start us, length us, event | category | flops | bytes accessed | tf_op | source)
XLA Modules:
  0.0 75.3 jit_solution(13485940774448427419)
XLA Ops:
  0.7 72.7 %shard_map.64 = f32[32,5120]{1,0:T(8,128)} custom-call(s32[1,1]{1,0:T(1,128)S(6)} %copy.7.counts, s32[1,512]{1,0:T(1,128)} %drows.1, s32[1,5120]{1,0:T(1,128)} %dcols.1, s32[5120]{0:T(1024)} %signs.1, bf16[512,512]{1,0:T(8,128)(2,1)} %a_hbm.1, bf16[512,5120]{1,0:T(8,128)(2,1)} %c_hbm.1), custom_call_target="tpu_custom_call" | custom-call | flops 5368709120 | bytes 5767168 | tf_op jit(solution)/shard_map/pallas_call | solution.py:402
  73.4 2.0 %broadcast_multiply_fusion = f32[32,5120]{1,0:T(8,128)} fusion(f32[32,5120]{1,0:T(8,128)} %shard_map.64), kind=kLoop, calls=%fused_computation | loop fusion | flops 163840 | bytes 1310720 | tf_op jit(solution)/shard_map/mul | solution.py:470

commit v3 on v2

--- a/solution.py
+++ b/solution.py
@@ -24,10 +24,11 @@
     cols = groups * GROUP * HBLK
 
     def kernel(
-        counts, drows, dcols, signs, a_hbm, c_hbm, out,
+        counts, drows_hbm, dcols_hbm, signs_hbm, a_hbm, c_hbm, out_hbm,
+        drows, dcols, signs, out,
         cbuf, abuf, a2, hmat, colterm, rowterm, rot, pk1, pk2, scl,
         rplane, rpx, rpy, rcore, ra, rb, rb2, stage2, shares, rz, gathered,
-        load_sem, s_pk, r_px, r_py, s_core, r_core, s_one, r_a, r_b,
+        load_sem, store_sem, s_pk, r_px, r_py, s_core, r_core, s_one, r_a, r_b,
         s_two, r_b2, s_z, r_z, s_out, r_out, s_pair, r_pair,
     ):
         i_me = lax.axis_index("inter")
@@ -75,6 +76,10 @@
 
         load_a = pltpu.make_async_copy(a_hbm, abuf, load_sem.at[groups])
         load_a.start()
+        load_signs = pltpu.make_async_copy(signs_hbm, signs, load_sem.at[groups + 1])
+        load_rows = pltpu.make_async_copy(drows_hbm, drows, load_sem.at[groups + 2])
+        load_cols = pltpu.make_async_copy(dcols_hbm, dcols, load_sem.at[groups + 3])
+        load_signs.start()
         width = GROUP * HBLK
 
         def load_c(g):
@@ -85,6 +90,8 @@
 
         for g in range(groups):
             load_c(g).start()
+        load_rows.start()
+        load_cols.start()
 
         first = lax.broadcasted_iota(jnp.int32, (HBLK, HBLK), 0)
         second = lax.broadcasted_iota(jnp.int32, (HBLK, HBLK), 1)
@@ -134,6 +141,8 @@
         def split(value):
             high = value.astype(BF16)
             return high, (value - high.astype(F32)).astype(BF16)
+
+        wide = pk1.shape[2]
 
         def rotate(g):
             load_c(g).wait()
@@ -151,7 +160,9 @@
                 turned = turned * weight
                 rot[block] = turned
                 peaks.append(jnp.max(jnp.abs(turned), axis=0, keepdims=True))
-            pk1[g] = jnp.concatenate(peaks + peaks, axis=0)
+            pk1[g] = jnp.concatenate(
+                [p[:, :wide] for p in peaks] + [p[:, wide:] for p in peaks], axis=0
+            )
 
             @pl.when(g == 0)
             def _():
@@ -197,6 +208,10 @@
 
             lax.fori_loop(0, HBLK // 8, piece, 0, unroll=4)
 
+        def keep(found):
+            scl[:, :wide] = found[:GROUP] + 1e-06
+            scl[:, wide:] = found[GROUP:] + 1e-06
+
         def scales(g):
             @pl.when(g == 0)
             def _():
@@ -204,14 +219,14 @@
                 top_peaks = pk1[0]
                 for k in range(len(plane)):
                     top_peaks = jnp.maximum(top_peaks, rplane[k])
-                scl[...] = top_peaks + 1e-06
+                keep(top_peaks)
 
             @pl.when(g > 0)
             def _():
                 wait_for(rpy.at[g], r_py.at[g])
-                scl[...] = jnp.maximum(
+                keep(jnp.maximum(
                     jnp.maximum(pk2[g], rpy[g, 0]), jnp.maximum(rpy[g, 1], rpy[g, 2])
-                ) + 1e-06
+                ))
 
         def encode_other(g, t):
             encode(g, t, other)
@@ -304,12 +319,17 @@
             wait_for(rz.at[g], r_out.at[g])
             put(half_of(g, core), half_of(g, core), s_pair.at[g], r_pair.at[g], sibling)
 
+        def store(g):
+            at = pl.ds(pl.multiple_of(g * width, width), width)
+            return pltpu.make_async_copy(out.at[:, at], out_hbm.at[:, at], store_sem.at[g])
+
         def deliver(g):
             wait_for(half_of(g, other), r_pair.at[g])
             for k in range(GROUP):
                 at = pl.ds(pl.multiple_of((g * GROUP + k) * HBLK, HBLK), HBLK)
                 for n in range(4):
                     out[8 * n:8 * n + 8, at] = gathered[g, (k % 2) * depth + 4 * (k // 2) + n]
+            store(g).start()
 
         def settle(g):
             @pl.when(g == 0)
@@ -361,15 +381,18 @@
 
             return carry
 
+        load_signs.wait()
         lax.fori_loop(0, groups, early, 0)
+        load_rows.wait()
+        load_cols.wait()
         dither_terms()
 
         def late(s, carry):
             before_pair(s + 2 * (groups - ahead), peaks_over_y)
             before_pair(s, scales)
             at_half(s, encode_other)
+            at_half(s - 1, first_ring)
             at_half(s, encode_own)
-            at_half(s - 1, first_ring)
             at_half(s - 4, first_ring_on)
             at_half(s - 7, second_ring)
             at_half(s - 9, second_sum)
@@ -380,9 +403,15 @@
 
         lax.fori_loop(0, 2 * groups + 15, late, 0)
 
+        def hand_out(g, carry):
+            deliver(g)
+            return carry
+
+        lax.fori_loop(0, groups, hand_out, 0)
+
         def finish(g, carry):
-            deliver(g)
             settle(g)
+            store(g).wait()
             return carry
 
         lax.fori_loop(0, groups, finish, 0)
@@ -404,14 +433,18 @@
         out_shape=jax.ShapeDtypeStruct((share, cols), F32),
         in_specs=[
             pl.BlockSpec(memory_space=pltpu.SMEM),
-            pl.BlockSpec(memory_space=pltpu.VMEM),
-            pl.BlockSpec(memory_space=pltpu.VMEM),
-            pl.BlockSpec(memory_space=pltpu.VMEM),
+            pl.BlockSpec(memory_space=pl.ANY),
+            pl.BlockSpec(memory_space=pl.ANY),
+            pl.BlockSpec(memory_space=pl.ANY),
             pl.BlockSpec(memory_space=pl.ANY),
             pl.BlockSpec(memory_space=pl.ANY),
         ],
-        out_specs=pl.BlockSpec(memory_space=pltpu.VMEM),
+        out_specs=pl.BlockSpec(memory_space=pl.ANY),
         scratch_shapes=[
+            vmem((1, hidden), jnp.int32),
+            vmem((1, cols), jnp.int32),
+            vmem((cols,), jnp.int32),
+            vmem((share, cols), F32),
             vmem((groups, tokens, GROUP * HBLK), BF16),
             vmem((tokens, hidden), BF16),
             vmem((2, hidden, tokens), BF16),
@@ -419,12 +452,12 @@
             vmem((cols, 128), F32),
             vmem((2, 8, hidden), F32),
             vmem((blocks, HBLK, hidden), F32),
-            vmem((groups, 8, hidden), F32),
-            vmem((groups, 8, hidden), F32),
-            vmem((8, hidden), F32),
-            vmem((SIDE * SIDE - 1, 8, hidden), F32),
-            vmem((groups, SIDE - 1, 8, hidden), F32),
-            vmem((groups, SIDE - 1, 8, hidden), F32),
+            vmem((groups, 8, hidden // 2), F32),
+            vmem((groups, 8, hidden // 2), F32),
+            vmem((GROUP, hidden), F32),
+            vmem((SIDE * SIDE - 1, 8, hidden // 2), F32),
+            vmem((groups, SIDE - 1, 8, hidden // 2), F32),
+            vmem((groups, SIDE - 1, 8, hidden // 2), F32),
             vmem((groups, 2, HBLK, hidden), F32),
             vmem((groups, 2, 2, HBLK // 2, 128), F32),
             vmem((groups, 2, 2, HBLK, 128), F32),
@@ -433,7 +466,8 @@
             vmem((groups, depth, 8, HBLK), F32),
             vmem((groups, depth - 1, 8, HBLK), F32),
             vmem((groups, CORES * depth, 8, HBLK), F32),
-            dma((groups + 1,)),
+            dma((groups + 4,)),
+            dma((groups,)),
             dma((groups, 2)),
             dma((groups,)),
             dma((groups,)),

time: 75.5 us -> 73.6 us (0.975)
  Pallas kernels: 72.7 us -> 70.8 us
    pallas_call x1, Pallas kernels: 72.7 us -> 70.8 us  [synchronize(): pl.pallas_call(make_kernel(depth, groups), out_shape=jax.ShapeDtypeStruct...]
where the time goes in v3:
time: 73.6 us; the launch traced here: 73.5 us
  Pallas kernels  70.8 us (96%)
  other arithmetic  1.97 us (3%)
    pallas_call x1, Pallas kernels, synchronize(): pl.pallas_call(make_kernel(depth, groups), out_shape=jax.ShapeDtypeStruct...  70.8 us
    mul x1, other arithmetic, body(): return summed * (1.0 / (math.sqrt(HBLK) * math.sqrt(mesh.size)))  1.97 us

profile of v3, /device:TPU:1, one launch (start us, length us, event | category | flops | bytes accessed | tf_op | source)
XLA Modules:
  0.0 73.5 jit_solution(14113822118277035313)
XLA Ops:
  0.7 70.8 %shard_map.64 = f32[32,5120]{1,0:T(8,128)} custom-call(s32[1,1]{1,0:T(1,128)S(6)} %copy.7.counts, s32[1,512]{1,0:T(1,128)} %drows_hbm.1, s32[1,5120]{1,0:T(1,128)} %dcols_hbm.1, s32[5120]{0:T(1024)} %signs_hbm.1, bf16[512,512]{1,0:T(8,128)(2,1)} %a_hbm.1, bf16[512,5120]{1,0:T(8,128)(2,1)} %c_hbm.1), custom_call_target="tpu_custom_call" | custom-call | flops 5368709120 | bytes 5767168 | tf_op jit(solution)/shard_map/pallas_call | solution.py:431
  71.5 2.0 %broadcast_multiply_fusion = f32[32,5120]{1,0:T(8,128)} fusion(f32[32,5120]{1,0:T(8,128)} %shard_map.64), kind=kLoop, calls=%fused_computation | loop fusion | flops 163840 | bytes 1310720 | tf_op jit(solution)/shard_map/mul | solution.py:504
